TPU v7x, 512 devices: a whole 4x8x8 slice. The times are simulated.
512 devices in a mesh: delay: 16 (over y, core), row: 32 (over z, x).
Axes of the slice: x: 4, y: 8, z: 8, core: 2. Of those that a mesh axis runs over, the one named last changes fastest.
Arguments:
- incident: bfloat16 [64, 4096], P(None, 'row'), may hold values from -12 to 12
- onset: int32 [64], replicated, may hold values from 0 to 2
- beta: float32 [4096], P('delay'), may hold values from 0.05 to 0.5
- inverse_block: bfloat16 [4096, 4096], P('row', 'delay'), may hold values from -0.0625 to 0.0625
- delay_blocks: bfloat16 [16, 4096, 4096], P('delay', None, 'row'), may hold values from -0.09375 to 0.09375
- history_sum: float32 [16, 64, 4096], P('delay', None, 'row'), may hold values from -12 to 12
Outputs:
- currents: bfloat16 [3, 64, 4096], P(None, None, 'delay')
- carried: float32 [16, 64, 4096], P('delay', None, 'row')
All inputs are finite; a program needn't handle non-finite values.
Results may differ from a plain program's by a relative error of at most 0.0056.
Values may be sent and summed in bfloat16 or wider, within the bound.
A program may use at most 64 MiB of HBM per device.

v0:
```python
import jax
import jax.numpy as jnp
from jax import lax
from jax.sharding import PartitionSpec as P

STEPS = 3


def broadcast(value, axis, root):
    return lax.dynamic_index_in_dim(lax.all_gather(value, axis), root, 0, keepdims=False)


def in_blocks(value, dim, devices):
    dims = value.shape
    blocks = value.reshape(*dims[:dim], devices, dims[dim] // devices, *dims[dim + 1 :])
    return jnp.moveaxis(blocks, dim, 0)


def sent_and_summed(value, axis, dim):
    devices = lax.axis_size(axis)
    blocks = lax.all_to_all(in_blocks(value, dim, devices), axis, 0, 0, tiled=True)
    return jnp.sum(blocks, axis=0)


def copy_for_each(value, axis):
    copies = jnp.broadcast_to(value, (lax.axis_size(axis), *value.shape))
    return lax.all_to_all(copies, axis, split_axis=0, concat_axis=0, tiled=True)


def joined_along(blocks, dim):
    blocks = jnp.moveaxis(blocks, 0, dim)
    dims = blocks.shape
    return blocks.reshape(*dims[:dim], dims[dim] * dims[dim + 1], *dims[dim + 2 :])


def gathered_copies(value, axis, dim):
    blocks = copy_for_each(value, axis)
    return joined_along(blocks, dim)


def passed_along(value, axis, by):
    devices = lax.axis_size(axis)
    pairs = [(i, i + by) for i in range(devices) if 0 <= i + by < devices]
    return lax.ppermute(value, axis, pairs)


def per_device(incident, onset, beta, inverse_block, delay_blocks, history_sum):
    future = history_sum[0]
    matrix = delay_blocks[0]
    incident_wide = incident.astype(jnp.float32)
    outputs = []
    for step_index in range(STEPS):
        offset_time = (step_index - onset).astype(jnp.float32)
        envelope = jnp.where(offset_time >= 0.0, jnp.exp(-((offset_time - 1.0) ** 2) / 4.0), 0.0)
        residual = (incident_wide * envelope[:, None] - future).astype(jnp.bfloat16)
        residual = broadcast(residual, "delay", 0)
        partial_sum = jnp.dot(residual, inverse_block, preferred_element_type=jnp.float32)
        solved = sent_and_summed(partial_sum, "row", 0)
        current = (solved / (1.0 + beta[None, :] * solved * solved)).astype(jnp.bfloat16)
        own_block = gathered_copies(current, "row", 0)
        gathered = lax.all_gather(own_block, "delay", axis=1, tiled=True)
        outputs.append(own_block)
        passed = passed_along(future, "delay", -1)
        future = passed + jnp.dot(gathered, matrix, preferred_element_type=jnp.float32)
    return (jnp.stack(outputs), future[None])


def solution(mesh):
    placed = (
        P(None, "row"),
        P(),
        P("delay"),
        P("row", "delay"),
        P("delay", None, "row"),
        P("delay", None, "row"),
    )
    return jax.shard_map(
        per_device,
        mesh=mesh,
        in_specs=placed,
        out_specs=(P(None, None, "delay"), P("delay", None, "row")),
        check_vma=False,
    )
```

profile of v0, /device:TPU:1, one launch (start us, length us, event | category | flops | bytes accessed | tf_op | source)
XLA Modules:
  0.0 199.1 jit_solution(9493592428893358727)
XLA Ops:
  0.6 0.0 copy-start
  0.6 0.8 compare_select_fusion.1
  1.4 0.9 fusion.12
  2.3 0.0 copy-start.1
  2.3 21.7 %all-gather = bf16[1024,128]{1,0:T(8,128)(2,1)S(1)} all-gather(bf16[64,128]{1,0:T(8,128)(2,1)S(1)} %fusion.12), channel_id=2, replica_groups=mesh['delay'=16,'row'=32] {'delay'}, dimensions={0}, use_global_device_ids=true | all-gather | bytes 278528 | tf_op jit(solution)/shard_map/all_gather | solution.py:10
  24.0 0.0 copy-done.1
  24.0 0.1 fusion.9
  24.1 0.1 copy.14
  24.2 19.6 %all_to_all.30 = f32[32,2,256]{2,1,0:T(2,128)S(1)} all-to-all(f32[32,2,256]{2,1,0:T(2,128)S(1)} %copy.14), channel_id=1, replica_groups=mesh['delay'=16,'row'=32] {'row'}, dimensions={0} | all-to-all | bytes 131072 | tf_op jit(solution)/shard_map/all_to_all | solution.py:21
  43.8 0.0 copy-start.4
  43.8 0.6 copy-done.4
  44.5 0.6 broadcast_in_dim.22
  45.1 0.0 copy-start.3
  45.1 4.0 %all-to-all-start.1 = ((bf16[32,2,256]{2,1,0:T(2,128)(2,1)}), bf16[32,2,256]{2,1,0:T(2,128)(2,1)S(1)}, u32[]{:S(2)}, u32[]{:S(2)}) async-start(bf16[32,2,256]{2,1,0:T(2,128)(2,1)} %broadcast_in_dim.22), calls=%async_computation.1 | async-start | bytes 65536 | tf_op jit(solution)/shard_map/all_to_all | solution.py:27
  49.1 0.0 copy-done.3
  49.1 3.5 %collective-permute-start = (f32[64,128]{1,0:T(8,128)S(1)}, f32[64,128]{1,0:T(8,128)S(1)}, u32[]{:S(2)}, u32[]{:S(2)}) collective-permute-start(f32[64,128]{1,0:T(8,128)S(1)} %bitcast.29), channel_id=1, source_target_pairs={{32,0},{64,32},{96,64},{128,96},{160,128},{192,160},{224,192},{256... | collective-permute-start | bytes 98312 | tf_op jit(solution)/shard_map/ppermute | solution.py:44
  52.6 5.1 %all-to-all-done.1 = bf16[32,2,256]{2,1,0:T(2,128)(2,1)S(1)} async-done(((bf16[32,2,256]{2,1,0:T(2,128)(2,1)}), bf16[32,2,256]{2,1,0:T(2,128)(2,1)S(1)}, u32[]{:S(2)}, u32[]{:S(2)}) %all-to-all-start.1) | async-done | bytes 32800 | tf_op jit(solution)/shard_map/all_to_all | solution.py:27
  57.7 0.0 copy-start.2
  57.8 18.9 %all_gather.29 = bf16[64,4096]{1,0:T(8,128)(2,1)S(1)} all-gather(bf16[64,256]{1,0:T(8,128)(2,1)S(1)} %reshape.26), channel_id=1, replica_groups=mesh['delay'=16,'row'=32] {'delay'}, dimensions={1}, use_global_device_ids=true | all-gather | bytes 557056 | tf_op jit(solution)/shard_map/all_gather | solution.py:61
  76.7 0.0 collective-permute-done
  76.7 0.0 copy-done
  76.7 0.0 copy-done.2
  76.7 0.3 fusion.14
  77.0 16.0 %all-gather.1 = bf16[1024,128]{1,0:T(8,128)(2,1)S(1)} all-gather(bf16[64,128]{1,0:T(8,128)(2,1)S(1)} %get-tuple-element.7), channel_id=3, replica_groups=mesh['delay'=16,'row'=32] {'delay'}, dimensions={0}, use_global_device_ids=true | all-gather | bytes 278528 | tf_op jit(solution)/shard_map/all_gather | solution.py:10
  93.1 0.1 fusion.7
  93.2 0.1 copy.16
  93.3 11.8 %all_to_all.31 = f32[32,2,256]{2,1,0:T(2,128)S(1)} all-to-all(f32[32,2,256]{2,1,0:T(2,128)S(1)} %copy.16), channel_id=1, replica_groups=mesh['delay'=16,'row'=32] {'row'}, dimensions={0} | all-to-all | bytes 131072 | tf_op jit(solution)/shard_map/all_to_all | solution.py:21
  105.2 0.6 broadcast_in_dim.23
  105.8 3.9 %all-to-all-start.3 = ((bf16[32,2,256]{2,1,0:T(2,128)(2,1)}), bf16[32,2,256]{2,1,0:T(2,128)(2,1)S(1)}, u32[]{:S(2)}, u32[]{:S(2)}) async-start(bf16[32,2,256]{2,1,0:T(2,128)(2,1)} %broadcast_in_dim.23), calls=%async_computation.3 | async-start | bytes 65536 | tf_op jit(solution)/shard_map/all_to_all | solution.py:27
  109.7 3.3 %collective-permute-start.1 = (f32[64,128]{1,0:T(8,128)S(1)}, f32[64,128]{1,0:T(8,128)S(1)}, u32[]{:S(2)}, u32[]{:S(2)}) collective-permute-start(f32[64,128]{1,0:T(8,128)S(1)} %get-tuple-element.8), channel_id=1, source_target_pairs={{32,0},{64,32},{96,64},{128,96},{160,128},{192,160},{224,192},{256... | collective-permute-start | bytes 98312 | tf_op jit(solution)/shard_map/ppermute | solution.py:44
  113.0 5.3 %all-to-all-done.3 = bf16[32,2,256]{2,1,0:T(2,128)(2,1)S(1)} async-done(((bf16[32,2,256]{2,1,0:T(2,128)(2,1)}), bf16[32,2,256]{2,1,0:T(2,128)(2,1)S(1)}, u32[]{:S(2)}, u32[]{:S(2)}) %all-to-all-start.3) | async-done | bytes 32800 | tf_op jit(solution)/shard_map/all_to_all | solution.py:27
  118.3 18.7 %all_gather.32 = bf16[64,4096]{1,0:T(8,128)(2,1)S(1)} all-gather(bf16[64,256]{1,0:T(8,128)(2,1)S(1)} %reshape.27), channel_id=1, replica_groups=mesh['delay'=16,'row'=32] {'delay'}, dimensions={1}, use_global_device_ids=true | all-gather | bytes 557056 | tf_op jit(solution)/shard_map/all_gather | solution.py:61
  137.0 0.3 fusion.2
  137.4 0.0 collective-permute-done.1
  137.4 0.1 fusion.16
  137.5 16.0 %all-gather.2 = bf16[1024,128]{1,0:T(8,128)(2,1)S(1)} all-gather(bf16[64,128]{1,0:T(8,128)(2,1)S(1)} %get-tuple-element.2), channel_id=4, replica_groups=mesh['delay'=16,'row'=32] {'delay'}, dimensions={0}, use_global_device_ids=true | all-gather | bytes 278528 | tf_op jit(solution)/shard_map/all_gather | solution.py:10
  153.5 0.1 fusion.5
  153.6 0.1 copy.18
  153.7 11.8 %all_to_all.32 = f32[32,2,256]{2,1,0:T(2,128)S(1)} all-to-all(f32[32,2,256]{2,1,0:T(2,128)S(1)} %copy.18), channel_id=1, replica_groups=mesh['delay'=16,'row'=32] {'row'}, dimensions={0} | all-to-all | bytes 131072 | tf_op jit(solution)/shard_map/all_to_all | solution.py:21
  165.6 0.6 broadcast_in_dim.24
  166.2 3.9 %all-to-all-start.5 = ((bf16[32,2,256]{2,1,0:T(2,128)(2,1)}), bf16[32,2,256]{2,1,0:T(2,128)(2,1)S(1)}, u32[]{:S(2)}, u32[]{:S(2)}) async-start(bf16[32,2,256]{2,1,0:T(2,128)(2,1)} %broadcast_in_dim.24), calls=%async_computation.5 | async-start | bytes 65536 | tf_op jit(solution)/shard_map/all_to_all | solution.py:27
  170.1 3.3 %collective-permute-start.2 = (f32[64,128]{1,0:T(8,128)S(1)}, f32[64,128]{1,0:T(8,128)S(1)}, u32[]{:S(2)}, u32[]{:S(2)}) collective-permute-start(f32[64,128]{1,0:T(8,128)S(1)} %get-tuple-element.3), channel_id=1, source_target_pairs={{32,0},{64,32},{96,64},{128,96},{160,128},{192,160},{224,192},{256... | collective-permute-start | bytes 98312 | tf_op jit(solution)/shard_map/ppermute | solution.py:44
  173.4 5.3 %all-to-all-done.5 = bf16[32,2,256]{2,1,0:T(2,128)(2,1)S(1)} async-done(((bf16[32,2,256]{2,1,0:T(2,128)(2,1)}), bf16[32,2,256]{2,1,0:T(2,128)(2,1)S(1)}, u32[]{:S(2)}, u32[]{:S(2)}) %all-to-all-start.5) | async-done | bytes 32800 | tf_op jit(solution)/shard_map/all_to_all | solution.py:27
  178.7 18.7 %all_gather.35 = bf16[64,4096]{1,0:T(8,128)(2,1)S(1)} all-gather(bf16[64,256]{1,0:T(8,128)(2,1)S(1)} %reshape.28), channel_id=1, replica_groups=mesh['delay'=16,'row'=32] {'delay'}, dimensions={1}, use_global_device_ids=true | all-gather | bytes 557056 | tf_op jit(solution)/shard_map/all_gather | solution.py:61
  197.5 0.3 fusion
  197.8 0.7 pad_maximum_fusion
  198.5 0.0 collective-permute-done.2
  198.5 0.6 add_bitcast_fusion
  (15 shorter events, 0.3 us)
Async XLA Ops:
  0.6 76.0 %copy-start = (bf16[1,4096,128]{2,1,0:T(8,128)(2,1)S(1)}, bf16[1,4096,128]{2,1,0:T(8,128)(2,1)}, u32[]{:S(2)}) copy-start(bf16[1,4096,128]{2,1,0:T(8,128)(2,1)} %param.10) | copy-start | bytes 3145732
  2.3 21.7 %copy-start.1 = (bf16[128,256]{1,0:T(8,128)(2,1)S(1)}, bf16[128,256]{1,0:T(8,128)(2,1)}, u32[]{:S(2)}) copy-start(bf16[128,256]{1,0:T(8,128)(2,1)} %param.9) | copy-start | bytes 196612
  43.8 0.7 copy-start.4
  45.1 4.0 %copy-start.3 = (f32[1,64,128]{2,1,0:T(8,128)S(1)}, f32[1,64,128]{2,1,0:T(8,128)}, u32[]{:S(2)}) copy-start(f32[1,64,128]{2,1,0:T(8,128)} %param.11) | copy-start | bytes 98308
  45.1 12.6 %all-to-all-start.1 = ((bf16[32,2,256]{2,1,0:T(2,128)(2,1)}), bf16[32,2,256]{2,1,0:T(2,128)(2,1)S(1)}, u32[]{:S(2)}, u32[]{:S(2)}) async-start(bf16[32,2,256]{2,1,0:T(2,128)(2,1)} %broadcast_in_dim.22), calls=%async_computation.1 | async-start | bytes 65536 | tf_op jit(solution)/shard_map/all_to_all | solution.py:27
  49.1 27.6 %collective-permute-start = (f32[64,128]{1,0:T(8,128)S(1)}, f32[64,128]{1,0:T(8,128)S(1)}, u32[]{:S(2)}, u32[]{:S(2)}) collective-permute-start(f32[64,128]{1,0:T(8,128)S(1)} %bitcast.29), channel_id=1, source_target_pairs={{32,0},{64,32},{96,64},{128,96},{160,128},{192,160},{224,192},{256... | collective-permute-start | bytes 98312 | tf_op jit(solution)/shard_map/ppermute | solution.py:44
  57.7 18.9 %copy-start.2 = (bf16[64,128]{1,0:T(8,128)(2,1)S(1)}, bf16[64,128]{1,0:T(8,128)(2,1)}, u32[]{:S(2)}) copy-start(bf16[64,128]{1,0:T(8,128)(2,1)} %param.6) | copy-start | bytes 49156
  105.8 12.5 %all-to-all-start.3 = ((bf16[32,2,256]{2,1,0:T(2,128)(2,1)}), bf16[32,2,256]{2,1,0:T(2,128)(2,1)S(1)}, u32[]{:S(2)}, u32[]{:S(2)}) async-start(bf16[32,2,256]{2,1,0:T(2,128)(2,1)} %broadcast_in_dim.23), calls=%async_computation.3 | async-start | bytes 65536 | tf_op jit(solution)/shard_map/all_to_all | solution.py:27
  109.7 27.7 %collective-permute-start.1 = (f32[64,128]{1,0:T(8,128)S(1)}, f32[64,128]{1,0:T(8,128)S(1)}, u32[]{:S(2)}, u32[]{:S(2)}) collective-permute-start(f32[64,128]{1,0:T(8,128)S(1)} %get-tuple-element.8), channel_id=1, source_target_pairs={{32,0},{64,32},{96,64},{128,96},{160,128},{192,160},{224,192},{256... | collective-permute-start | bytes 98312 | tf_op jit(solution)/shard_map/ppermute | solution.py:44
  166.2 12.5 %all-to-all-start.5 = ((bf16[32,2,256]{2,1,0:T(2,128)(2,1)}), bf16[32,2,256]{2,1,0:T(2,128)(2,1)S(1)}, u32[]{:S(2)}, u32[]{:S(2)}) async-start(bf16[32,2,256]{2,1,0:T(2,128)(2,1)} %broadcast_in_dim.24), calls=%async_computation.5 | async-start | bytes 65536 | tf_op jit(solution)/shard_map/all_to_all | solution.py:27
  170.1 28.4 %collective-permute-start.2 = (f32[64,128]{1,0:T(8,128)S(1)}, f32[64,128]{1,0:T(8,128)S(1)}, u32[]{:S(2)}, u32[]{:S(2)}) collective-permute-start(f32[64,128]{1,0:T(8,128)S(1)} %get-tuple-element.3), channel_id=1, source_target_pairs={{32,0},{64,32},{96,64},{128,96},{160,128},{192,160},{224,192},{256... | collective-permute-start | bytes 98312 | tf_op jit(solution)/shard_map/ppermute | solution.py:44
where the time goes:
time: 200 us; the launch traced here: 199 us
  blocking collectives  153 us (76%)
  starting transfers between devices  21.8 us (11%)
  waiting for transfers between devices  15.7 us (8%)
  other arithmetic  3.13 us (2%)
  local copies, waits for them, and re-layouts  2.87 us (1%)
    all_gather x3, blocking collectives, per_device(): gathered = lax.all_gather(own_block, 'delay', axis=1, tiled=True)  56.4 us
    all_gather x3, blocking collectives, broadcast(): lax.all_gather(value, axis)  53.8 us
    all_to_all x3, blocking collectives, sent_and_summed(): lax.all_to_all(in_blocks(value, dim, devices), axis, 0, 0, tiled=True)  43.3 us
    all_to_all x3, waiting for transfers between devices, copy_for_each(): return lax.all_to_all(copies, axis, split_axis=0, concat_axis=0, tiled=True)  15.7 us
    all_to_all x3, starting transfers between devices, copy_for_each(): return lax.all_to_all(copies, axis, split_axis=0, concat_axis=0, tiled=True)  11.7 us
    ppermute x3, starting transfers between devices, passed_along(): return lax.ppermute(value, axis, pairs)  10.1 us
  transfers between devices with their start and end apart: 6, of which 3 were waited for; matrix products, arithmetic and copies ran while one was open for 1% of the time, Pallas kernels for 0%

commit v1 on v0

--- a/solution.py
+++ b/solution.py
@@ -58,7 +58,33 @@
         solved = sent_and_summed(partial_sum, "row", 0)
         current = (solved / (1.0 + beta[None, :] * solved * solved)).astype(jnp.bfloat16)
         own_block = gathered_copies(current, "row", 0)
-        gathered = lax.all_gather(own_block, "delay", axis=1, tiled=True)
+
+        def replace_the_pipes(xin):
+            device_axis = "delay"
+            prior, current_value, before = (
+                lax.axis_size(device_axis),
+                lax.axis_index(device_axis),
+                xin.shape[1],
+            )
+            slots = tuple(((k, (k + 1) % prior) for k in range(prior)))
+            leaves = tuple(((k, (k - 1) % prior) for k in range(prior)))
+            lower = jnp.zeros((*xin.shape[:1], prior * before, *xin.shape[2:]), xin.dtype)
+            lower = lax.dynamic_update_slice_in_dim(lower, xin, current_value * before, axis=1)
+            inter = left_arr = xin
+            piece_now = prior // 2
+            for nth in range(1, piece_now + 1):
+                inter = lax.ppermute(inter, device_axis, slots)
+                lower = lax.dynamic_update_slice_in_dim(
+                    lower, inter, (current_value - nth) % prior * before, axis=1
+                )
+                if nth < prior - piece_now:
+                    left_arr = lax.ppermute(left_arr, device_axis, leaves)
+                    lower = lax.dynamic_update_slice_in_dim(
+                        lower, left_arr, (current_value + nth) % prior * before, axis=1
+                    )
+            return lower
+
+        gathered = replace_the_pipes(own_block)
         outputs.append(own_block)
         passed = passed_along(future, "delay", -1)
         future = passed + jnp.dot(gathered, matrix, preferred_element_type=jnp.float32)

time: 200 us -> 255 us (1.27)
  starting transfers between devices: 21.8 us -> 94.7 us
  blocking collectives: 153 us -> 102 us
  waiting for transfers between devices: 15.7 us -> 46.9 us
    ppermute x0 -> x45, starting transfers between devices: none -> 72.9 us  [the longest x21 44.6 us: replace_the_pipes(): left_arr = lax.ppermute(left_arr, device_axis, leaves)]
    all_gather x3 -> x0, blocking collectives: 56.4 us -> none  [per_device(): gathered = lax.all_gather(own_block, 'delay', axis=1, tiled=True)]
    ppermute x0 -> x45, waiting for transfers between devices: none -> 31.4 us  [the longest x24 27.7 us: replace_the_pipes(): inter = lax.ppermute(inter, device_axis, slots)]
    all_gather x3, blocking collectives: 53.8 us -> 58.8 us  [broadcast(): lax.all_gather(value, axis)]
  transfers between devices with their start and end apart: 6 -> 51, of which waited for: 3 -> 44; matrix products, arithmetic and copies ran while one was open for 1% -> 0% of each run, Pallas kernels for 0% -> 0%
where the time goes in v1:
time: 255 us; the launch traced here: 253 us
  blocking collectives  102 us (40%)
  starting transfers between devices  94.7 us (37%)
  waiting for transfers between devices  46.9 us (18%)
  local copies, waits for them, and re-layouts  3.2 us (1%)
    all_gather x3, blocking collectives, broadcast(): lax.all_gather(value, axis)  58.8 us
    ppermute x21, starting transfers between devices, replace_the_pipes(): left_arr = lax.ppermute(left_arr, device_axis, leaves)  44.6 us
    all_to_all x3, blocking collectives, sent_and_summed(): lax.all_to_all(in_blocks(value, dim, devices), axis, 0, 0, tiled=True)  43.3 us
    ppermute x24, starting transfers between devices, replace_the_pipes(): inter = lax.ppermute(inter, device_axis, slots)  28.3 us
    ppermute x24, waiting for transfers between devices, replace_the_pipes(): inter = lax.ppermute(inter, device_axis, slots)  27.7 us
    all_to_all x3, waiting for transfers between devices, copy_for_each(): return lax.all_to_all(copies, axis, split_axis=0, concat_axis=0, tiled=True)  15.5 us
    all_to_all x3, starting transfers between devices, copy_for_each(): return lax.all_to_all(copies, axis, split_axis=0, concat_axis=0, tiled=True)  11.7 us
    ppermute x3, starting transfers between devices, passed_along(): return lax.ppermute(value, axis, pairs)  10.1 us
  transfers between devices with their start and end apart: 51, of which 44 were waited for; matrix products, arithmetic and copies ran while one was open for 0% of the time, Pallas kernels for 0%

profile of v1, /device:TPU:1, one launch (start us, length us, event | category | flops | bytes accessed | tf_op | source)
XLA Modules:
  0.0 252.5 jit_solution(7011252682303449512)
XLA Ops:
  0.6 0.8 compare_select_fusion
  1.4 0.9 fusion.11
  2.3 21.7 %all-gather = bf16[1024,128]{1,0:T(8,128)(2,1)S(1)} all-gather(bf16[64,128]{1,0:T(8,128)(2,1)S(1)} %fusion.11), channel_id=2, replica_groups=mesh['delay'=16,'row'=32] {'delay'}, dimensions={0}, use_global_device_ids=true | all-gather | bytes 278528 | tf_op jit(solution)/shard_map/all_gather | solution.py:10
  24.2 19.6 %all_to_all.30 = f32[32,2,256]{2,1,0:T(2,128)S(1)} all-to-all(f32[32,2,256]{2,1,0:T(2,128)S(1)} %copy.14), channel_id=1, replica_groups=mesh['delay'=16,'row'=32] {'row'}, dimensions={0} | all-to-all | bytes 131072 | tf_op jit(solution)/shard_map/all_to_all | solution.py:21
  45.1 4.0 %all-to-all-start.1 = ((bf16[32,2,256]{2,1,0:T(2,128)(2,1)}), bf16[32,2,256]{2,1,0:T(2,128)(2,1)S(1)}, u32[]{:S(2)}, u32[]{:S(2)}) async-start(bf16[32,2,256]{2,1,0:T(2,128)(2,1)} %broadcast_in_dim.22), calls=%async_computation.1 | async-start | bytes 65536 | tf_op jit(solution)/shard_map/all_to_all | solution.py:27
  49.1 3.5 %collective-permute-start = (f32[64,128]{1,0:T(8,128)S(1)}, f32[64,128]{1,0:T(8,128)S(1)}, u32[]{:S(2)}, u32[]{:S(2)}) collective-permute-start(f32[64,128]{1,0:T(8,128)S(1)} %bitcast.31), channel_id=1, source_target_pairs={{32,0},{64,32},{96,64},{128,96},{160,128},{192,160},{224,192},{256... | collective-permute-start | bytes 98312 | tf_op jit(solution)/shard_map/ppermute | solution.py:44
  52.9 4.9 %all-to-all-done.1 = bf16[32,2,256]{2,1,0:T(2,128)(2,1)S(1)} async-done(((bf16[32,2,256]{2,1,0:T(2,128)(2,1)}), bf16[32,2,256]{2,1,0:T(2,128)(2,1)S(1)}, u32[]{:S(2)}, u32[]{:S(2)}) %all-to-all-start.1) | async-done | bytes 32800 | tf_op jit(solution)/shard_map/all_to_all | solution.py:27
  57.7 2.5 collective-permute-start.1
  60.5 0.7 collective-permute-done.1
  61.2 2.3 collective-permute-start.3
  63.6 1.5 collective-permute-start.4
  65.0 0.7 collective-permute-done.3
  65.7 1.2 collective-permute-start.5
  66.9 2.7 %collective-permute-start.6 = (bf16[64,256]{1,0:T(8,128)(2,1)S(1)}, bf16[64,256]{1,0:T(8,128)(2,1)S(1)}, u32[]{:S(2)}, u32[]{:S(2)}) collective-permute-start(bf16[64,256]{1,0:T(8,128)(2,1)S(1)} %collective-permute-done.4), channel_id=1, source_target_pairs={{0,480},{32,0},{64,32},{96,64},{128,96},{160,128},{192,160},{224,1... | collective-permute-start | bytes 98312 | tf_op jit(solution)/shard_map/ppermute | solution.py:81
  69.6 0.7 collective-permute-done.5
  70.4 3.7 %collective-permute-start.8 = (bf16[64,256]{1,0:T(8,128)(2,1)S(1)}, bf16[64,256]{1,0:T(8,128)(2,1)S(1)}, u32[]{:S(2)}, u32[]{:S(2)}) collective-permute-start(bf16[64,256]{1,0:T(8,128)(2,1)S(1)} %collective-permute-done.6), channel_id=1, source_target_pairs={{0,480},{32,0},{64,32},{96,64},{128,96},{160,128},{192,160},{224,1... | collective-permute-start | bytes 98312 | tf_op jit(solution)/shard_map/ppermute | solution.py:81
  74.1 0.7 collective-permute-done.7
  75.0 3.7 %collective-permute-start.10 = (bf16[64,256]{1,0:T(8,128)(2,1)S(1)}, bf16[64,256]{1,0:T(8,128)(2,1)S(1)}, u32[]{:S(2)}, u32[]{:S(2)}) collective-permute-start(bf16[64,256]{1,0:T(8,128)(2,1)S(1)} %collective-permute-done.8), channel_id=1, source_target_pairs={{0,480},{32,0},{64,32},{96,64},{128,96},{160,128},{192,160},{224,1... | collective-permute-start | bytes 98312 | tf_op jit(solution)/shard_map/ppermute | solution.py:81
  78.7 0.7 collective-permute-done.9
  79.5 3.7 %collective-permute-start.12 = (bf16[64,256]{1,0:T(8,128)(2,1)S(1)}, bf16[64,256]{1,0:T(8,128)(2,1)S(1)}, u32[]{:S(2)}, u32[]{:S(2)}) collective-permute-start(bf16[64,256]{1,0:T(8,128)(2,1)S(1)} %collective-permute-done.10), channel_id=1, source_target_pairs={{0,480},{32,0},{64,32},{96,64},{128,96},{160,128},{192,160},{224,1... | collective-permute-start | bytes 98312 | tf_op jit(solution)/shard_map/ppermute | solution.py:81
  83.2 0.7 collective-permute-done.11
  84.1 3.7 %collective-permute-start.14 = (bf16[64,256]{1,0:T(8,128)(2,1)S(1)}, bf16[64,256]{1,0:T(8,128)(2,1)S(1)}, u32[]{:S(2)}, u32[]{:S(2)}) collective-permute-start(bf16[64,256]{1,0:T(8,128)(2,1)S(1)} %collective-permute-done.12), channel_id=1, source_target_pairs={{0,480},{32,0},{64,32},{96,64},{128,96},{160,128},{192,160},{224,1... | collective-permute-start | bytes 98312 | tf_op jit(solution)/shard_map/ppermute | solution.py:81
  87.8 0.7 collective-permute-done.13
  88.6 4.4 %collective-permute-done.15 = bf16[64,256]{1,0:T(8,128)(2,1)S(1)} collective-permute-done((bf16[64,256]{1,0:T(8,128)(2,1)S(1)}, bf16[64,256]{1,0:T(8,128)(2,1)S(1)}, u32[]{:S(2)}, u32[]{:S(2)}) %collective-permute-start.15) | collective-permute-done | bytes 32800 | tf_op jit(solution)/shard_map/ppermute | solution.py:76
  93.4 18.6 %all-gather.1 = bf16[1024,128]{1,0:T(8,128)(2,1)S(1)} all-gather(bf16[64,128]{1,0:T(8,128)(2,1)S(1)} %get-tuple-element.5), channel_id=3, replica_groups=mesh['delay'=16,'row'=32] {'delay'}, dimensions={0}, use_global_device_ids=true | all-gather | bytes 278528 | tf_op jit(solution)/shard_map/all_gather | solution.py:10
  112.1 11.8 %all_to_all.31 = f32[32,2,256]{2,1,0:T(2,128)S(1)} all-to-all(f32[32,2,256]{2,1,0:T(2,128)S(1)} %copy.16), channel_id=1, replica_groups=mesh['delay'=16,'row'=32] {'row'}, dimensions={0} | all-to-all | bytes 131072 | tf_op jit(solution)/shard_map/all_to_all | solution.py:21
  124.7 3.9 %all-to-all-start.3 = ((bf16[32,2,256]{2,1,0:T(2,128)(2,1)}), bf16[32,2,256]{2,1,0:T(2,128)(2,1)S(1)}, u32[]{:S(2)}, u32[]{:S(2)}) async-start(bf16[32,2,256]{2,1,0:T(2,128)(2,1)} %broadcast_in_dim.23), calls=%async_computation.3 | async-start | bytes 65536 | tf_op jit(solution)/shard_map/all_to_all | solution.py:27
  128.5 3.3 %collective-permute-start.16 = (f32[64,128]{1,0:T(8,128)S(1)}, f32[64,128]{1,0:T(8,128)S(1)}, u32[]{:S(2)}, u32[]{:S(2)}) collective-permute-start(f32[64,128]{1,0:T(8,128)S(1)} %get-tuple-element.6), channel_id=1, source_target_pairs={{32,0},{64,32},{96,64},{128,96},{160,128},{192,160},{224,192},{256... | collective-permute-start | bytes 98312 | tf_op jit(solution)/shard_map/ppermute | solution.py:44
  131.9 5.3 %all-to-all-done.3 = bf16[32,2,256]{2,1,0:T(2,128)(2,1)S(1)} async-done(((bf16[32,2,256]{2,1,0:T(2,128)(2,1)}), bf16[32,2,256]{2,1,0:T(2,128)(2,1)S(1)}, u32[]{:S(2)}, u32[]{:S(2)}) %all-to-all-start.3) | async-done | bytes 32800 | tf_op jit(solution)/shard_map/all_to_all | solution.py:27
  137.2 4.1 %collective-permute-start.17 = (bf16[64,256]{1,0:T(8,128)(2,1)S(1)}, bf16[64,256]{1,0:T(8,128)(2,1)S(1)}, u32[]{:S(2)}, u32[]{:S(2)}) collective-permute-start(bf16[64,256]{1,0:T(8,128)(2,1)S(1)} %reshape.27), channel_id=1, source_target_pairs={{0,32},{32,64},{64,96},{96,128},{128,160},{160,192},{192,224},{224... | collective-permute-start | bytes 98312 | tf_op jit(solution)/shard_map/ppermute | solution.py:76
  141.4 1.0 collective-permute-done.17
  142.4 2.3 collective-permute-start.19
  144.7 1.0 collective-permute-done.19
  145.7 2.3 collective-permute-start.21
  148.9 0.7 collective-permute-done.21
  149.5 1.8 collective-permute-start.23
  151.7 1.8 collective-permute-start.24
  153.4 0.7 collective-permute-done.23
  155.0 3.0 %collective-permute-start.26 = (bf16[64,256]{1,0:T(8,128)(2,1)S(1)}, bf16[64,256]{1,0:T(8,128)(2,1)S(1)}, u32[]{:S(2)}, u32[]{:S(2)}) collective-permute-start(bf16[64,256]{1,0:T(8,128)(2,1)S(1)} %collective-permute-done.24), channel_id=1, source_target_pairs={{0,480},{32,0},{64,32},{96,64},{128,96},{160,128},{192,160},{224,1... | collective-permute-start | bytes 98312 | tf_op jit(solution)/shard_map/ppermute | solution.py:81
  158.0 0.7 collective-permute-done.25
  158.8 3.7 %collective-permute-start.28 = (bf16[64,256]{1,0:T(8,128)(2,1)S(1)}, bf16[64,256]{1,0:T(8,128)(2,1)S(1)}, u32[]{:S(2)}, u32[]{:S(2)}) collective-permute-start(bf16[64,256]{1,0:T(8,128)(2,1)S(1)} %collective-permute-done.26), channel_id=1, source_target_pairs={{0,480},{32,0},{64,32},{96,64},{128,96},{160,128},{192,160},{224,1... | collective-permute-start | bytes 98312 | tf_op jit(solution)/shard_map/ppermute | solution.py:81
  162.5 0.7 collective-permute-done.27
  163.4 3.7 %collective-permute-start.30 = (bf16[64,256]{1,0:T(8,128)(2,1)S(1)}, bf16[64,256]{1,0:T(8,128)(2,1)S(1)}, u32[]{:S(2)}, u32[]{:S(2)}) collective-permute-start(bf16[64,256]{1,0:T(8,128)(2,1)S(1)} %collective-permute-done.28), channel_id=1, source_target_pairs={{0,480},{32,0},{64,32},{96,64},{128,96},{160,128},{192,160},{224,1... | collective-permute-start | bytes 98312 | tf_op jit(solution)/shard_map/ppermute | solution.py:81
  167.1 0.7 collective-permute-done.29
  168.0 4.4 %collective-permute-done.31 = bf16[64,256]{1,0:T(8,128)(2,1)S(1)} collective-permute-done((bf16[64,256]{1,0:T(8,128)(2,1)S(1)}, bf16[64,256]{1,0:T(8,128)(2,1)S(1)}, u32[]{:S(2)}, u32[]{:S(2)}) %collective-permute-start.31) | collective-permute-done | bytes 32800 | tf_op jit(solution)/shard_map/ppermute | solution.py:76
  172.7 18.6 %all-gather.2 = bf16[1024,128]{1,0:T(8,128)(2,1)S(1)} all-gather(bf16[64,128]{1,0:T(8,128)(2,1)S(1)} %get-tuple-element.7), channel_id=4, replica_groups=mesh['delay'=16,'row'=32] {'delay'}, dimensions={0}, use_global_device_ids=true | all-gather | bytes 278528 | tf_op jit(solution)/shard_map/all_gather | solution.py:10
  191.4 11.8 %all_to_all.32 = f32[32,2,256]{2,1,0:T(2,128)S(1)} all-to-all(f32[32,2,256]{2,1,0:T(2,128)S(1)} %copy.18), channel_id=1, replica_groups=mesh['delay'=16,'row'=32] {'row'}, dimensions={0} | all-to-all | bytes 131072 | tf_op jit(solution)/shard_map/all_to_all | solution.py:21
  203.9 3.9 %all-to-all-start.5 = ((bf16[32,2,256]{2,1,0:T(2,128)(2,1)}), bf16[32,2,256]{2,1,0:T(2,128)(2,1)S(1)}, u32[]{:S(2)}, u32[]{:S(2)}) async-start(bf16[32,2,256]{2,1,0:T(2,128)(2,1)} %broadcast_in_dim.24), calls=%async_computation.5 | async-start | bytes 65536 | tf_op jit(solution)/shard_map/all_to_all | solution.py:27
  207.9 3.3 %collective-permute-start.32 = (f32[64,128]{1,0:T(8,128)S(1)}, f32[64,128]{1,0:T(8,128)S(1)}, u32[]{:S(2)}, u32[]{:S(2)}) collective-permute-start(f32[64,128]{1,0:T(8,128)S(1)} %get-tuple-element.8), channel_id=1, source_target_pairs={{32,0},{64,32},{96,64},{128,96},{160,128},{192,160},{224,192},{256... | collective-permute-start | bytes 98312 | tf_op jit(solution)/shard_map/ppermute | solution.py:44
  211.2 5.3 %all-to-all-done.5 = bf16[32,2,256]{2,1,0:T(2,128)(2,1)S(1)} async-done(((bf16[32,2,256]{2,1,0:T(2,128)(2,1)}), bf16[32,2,256]{2,1,0:T(2,128)(2,1)S(1)}, u32[]{:S(2)}, u32[]{:S(2)}) %all-to-all-start.5) | async-done | bytes 32800 | tf_op jit(solution)/shard_map/all_to_all | solution.py:27
  216.5 4.1 %collective-permute-start.33 = (bf16[64,256]{1,0:T(8,128)(2,1)S(1)}, bf16[64,256]{1,0:T(8,128)(2,1)S(1)}, u32[]{:S(2)}, u32[]{:S(2)}) collective-permute-start(bf16[64,256]{1,0:T(8,128)(2,1)S(1)} %reshape.28), channel_id=1, source_target_pairs={{0,32},{32,64},{64,96},{96,128},{128,160},{160,192},{192,224},{224... | collective-permute-start | bytes 98312 | tf_op jit(solution)/shard_map/ppermute | solution.py:76
  221.6 2.3 collective-permute-start.35
  224.0 1.0 collective-permute-done.35
  225.0 2.3 collective-permute-start.37
  228.1 0.7 collective-permute-done.37
  228.8 1.8 collective-permute-start.39
  230.9 1.8 collective-permute-start.40
  234.3 3.0 %collective-permute-start.42 = (bf16[64,256]{1,0:T(8,128)(2,1)S(1)}, bf16[64,256]{1,0:T(8,128)(2,1)S(1)}, u32[]{:S(2)}, u32[]{:S(2)}) collective-permute-start(bf16[64,256]{1,0:T(8,128)(2,1)S(1)} %collective-permute-done.40), channel_id=1, source_target_pairs={{0,480},{32,0},{64,32},{96,64},{128,96},{160,128},{192,160},{224,1... | collective-permute-start | bytes 98312 | tf_op jit(solution)/shard_map/ppermute | solution.py:81
  237.2 0.7 collective-permute-done.41
  238.1 3.7 %collective-permute-start.44 = (bf16[64,256]{1,0:T(8,128)(2,1)S(1)}, bf16[64,256]{1,0:T(8,128)(2,1)S(1)}, u32[]{:S(2)}, u32[]{:S(2)}) collective-permute-start(bf16[64,256]{1,0:T(8,128)(2,1)S(1)} %collective-permute-done.42), channel_id=1, source_target_pairs={{0,480},{32,0},{64,32},{96,64},{128,96},{160,128},{192,160},{224,1... | collective-permute-start | bytes 98312 | tf_op jit(solution)/shard_map/ppermute | solution.py:81
  242.7 3.7 %collective-permute-start.46 = (bf16[64,256]{1,0:T(8,128)(2,1)S(1)}, bf16[64,256]{1,0:T(8,128)(2,1)S(1)}, u32[]{:S(2)}, u32[]{:S(2)}) collective-permute-start(bf16[64,256]{1,0:T(8,128)(2,1)S(1)} %collective-permute-done.44), channel_id=1, source_target_pairs={{0,480},{32,0},{64,32},{96,64},{128,96},{160,128},{192,160},{224,1... | collective-permute-start | bytes 98312 | tf_op jit(solution)/shard_map/ppermute | solution.py:81
  246.4 0.7 collective-permute-done.45
  247.2 4.4 %collective-permute-done.47 = bf16[64,256]{1,0:T(8,128)(2,1)S(1)} collective-permute-done((bf16[64,256]{1,0:T(8,128)(2,1)S(1)}, bf16[64,256]{1,0:T(8,128)(2,1)S(1)}, u32[]{:S(2)}, u32[]{:S(2)}) %collective-permute-start.47) | collective-permute-done | bytes 32800 | tf_op jit(solution)/shard_map/ppermute | solution.py:76
  251.6 0.9 fusion
  (135 shorter events, 13.1 us)
Async XLA Ops:
  0.6 92.4 %copy-start = (bf16[1,4096,128]{2,1,0:T(8,128)(2,1)S(1)}, bf16[1,4096,128]{2,1,0:T(8,128)(2,1)}, u32[]{:S(2)}) copy-start(bf16[1,4096,128]{2,1,0:T(8,128)(2,1)} %param.10) | copy-start | bytes 3145732
  2.3 21.7 %copy-start.1 = (bf16[128,256]{1,0:T(8,128)(2,1)S(1)}, bf16[128,256]{1,0:T(8,128)(2,1)}, u32[]{:S(2)}) copy-start(bf16[128,256]{1,0:T(8,128)(2,1)} %param.9) | copy-start | bytes 196612
  43.8 0.7 copy-start.4
  45.1 4.0 %copy-start.3 = (f32[1,64,128]{2,1,0:T(8,128)S(1)}, f32[1,64,128]{2,1,0:T(8,128)}, u32[]{:S(2)}) copy-start(f32[1,64,128]{2,1,0:T(8,128)} %param.11) | copy-start | bytes 98308
  45.1 12.6 %all-to-all-start.1 = ((bf16[32,2,256]{2,1,0:T(2,128)(2,1)}), bf16[32,2,256]{2,1,0:T(2,128)(2,1)S(1)}, u32[]{:S(2)}, u32[]{:S(2)}) async-start(bf16[32,2,256]{2,1,0:T(2,128)(2,1)} %broadcast_in_dim.22), calls=%async_computation.1 | async-start | bytes 65536 | tf_op jit(solution)/shard_map/all_to_all | solution.py:27
  49.1 43.9 %collective-permute-start = (f32[64,128]{1,0:T(8,128)S(1)}, f32[64,128]{1,0:T(8,128)S(1)}, u32[]{:S(2)}, u32[]{:S(2)}) collective-permute-start(f32[64,128]{1,0:T(8,128)S(1)} %bitcast.31), channel_id=1, source_target_pairs={{32,0},{64,32},{96,64},{128,96},{160,128},{192,160},{224,192},{256... | collective-permute-start | bytes 98312 | tf_op jit(solution)/shard_map/ppermute | solution.py:44
  57.7 3.5 %collective-permute-start.1 = (bf16[64,256]{1,0:T(8,128)(2,1)S(1)}, bf16[64,256]{1,0:T(8,128)(2,1)S(1)}, u32[]{:S(2)}, u32[]{:S(2)}) collective-permute-start(bf16[64,256]{1,0:T(8,128)(2,1)S(1)} %reshape.26), channel_id=1, source_target_pairs={{0,32},{32,64},{64,96},{96,128},{128,160},{160,192},{192,224},{224... | collective-permute-start | bytes 98312 | tf_op jit(solution)/shard_map/ppermute | solution.py:76
  60.2 3.3 %collective-permute-start.2 = (bf16[64,256]{1,0:T(8,128)(2,1)S(1)}, bf16[64,256]{1,0:T(8,128)(2,1)S(1)}, u32[]{:S(2)}, u32[]{:S(2)}) collective-permute-start(bf16[64,256]{1,0:T(8,128)(2,1)S(1)} %reshape.26), channel_id=1, source_target_pairs={{0,480},{32,0},{64,32},{96,64},{128,96},{160,128},{192,160},{224,1... | collective-permute-start | bytes 98312 | tf_op jit(solution)/shard_map/ppermute | solution.py:81
  61.2 4.5 %collective-permute-start.3 = (bf16[64,256]{1,0:T(8,128)(2,1)S(1)}, bf16[64,256]{1,0:T(8,128)(2,1)S(1)}, u32[]{:S(2)}, u32[]{:S(2)}) collective-permute-start(bf16[64,256]{1,0:T(8,128)(2,1)S(1)} %collective-permute-done.1), channel_id=1, source_target_pairs={{0,32},{32,64},{64,96},{96,128},{128,160},{160,192},{192,224},{224... | collective-permute-start | bytes 98312 | tf_op jit(solution)/shard_map/ppermute | solution.py:76
  63.6 3.3 %collective-permute-start.4 = (bf16[64,256]{1,0:T(8,128)(2,1)S(1)}, bf16[64,256]{1,0:T(8,128)(2,1)S(1)}, u32[]{:S(2)}, u32[]{:S(2)}) collective-permute-start(bf16[64,256]{1,0:T(8,128)(2,1)S(1)} %collective-permute-done.2), channel_id=1, source_target_pairs={{0,480},{32,0},{64,32},{96,64},{128,96},{160,128},{192,160},{224,1... | collective-permute-start | bytes 98312 | tf_op jit(solution)/shard_map/ppermute | solution.py:81
  65.7 4.6 %collective-permute-start.5 = (bf16[64,256]{1,0:T(8,128)(2,1)S(1)}, bf16[64,256]{1,0:T(8,128)(2,1)S(1)}, u32[]{:S(2)}, u32[]{:S(2)}) collective-permute-start(bf16[64,256]{1,0:T(8,128)(2,1)S(1)} %collective-permute-done.3), channel_id=1, source_target_pairs={{0,32},{32,64},{64,96},{96,128},{128,160},{160,192},{192,224},{224... | collective-permute-start | bytes 98312 | tf_op jit(solution)/shard_map/ppermute | solution.py:76
  66.9 3.5 %collective-permute-start.6 = (bf16[64,256]{1,0:T(8,128)(2,1)S(1)}, bf16[64,256]{1,0:T(8,128)(2,1)S(1)}, u32[]{:S(2)}, u32[]{:S(2)}) collective-permute-start(bf16[64,256]{1,0:T(8,128)(2,1)S(1)} %collective-permute-done.4), channel_id=1, source_target_pairs={{0,480},{32,0},{64,32},{96,64},{128,96},{160,128},{192,160},{224,1... | collective-permute-start | bytes 98312 | tf_op jit(solution)/shard_map/ppermute | solution.py:81
  70.3 4.6 %collective-permute-start.7 = (bf16[64,256]{1,0:T(8,128)(2,1)S(1)}, bf16[64,256]{1,0:T(8,128)(2,1)S(1)}, u32[]{:S(2)}, u32[]{:S(2)}) collective-permute-start(bf16[64,256]{1,0:T(8,128)(2,1)S(1)} %collective-permute-done.5), channel_id=1, source_target_pairs={{0,32},{32,64},{64,96},{96,128},{128,160},{160,192},{192,224},{224... | collective-permute-start | bytes 98312 | tf_op jit(solution)/shard_map/ppermute | solution.py:76
  70.4 4.6 %collective-permute-start.8 = (bf16[64,256]{1,0:T(8,128)(2,1)S(1)}, bf16[64,256]{1,0:T(8,128)(2,1)S(1)}, u32[]{:S(2)}, u32[]{:S(2)}) collective-permute-start(bf16[64,256]{1,0:T(8,128)(2,1)S(1)} %collective-permute-done.6), channel_id=1, source_target_pairs={{0,480},{32,0},{64,32},{96,64},{128,96},{160,128},{192,160},{224,1... | collective-permute-start | bytes 98312 | tf_op jit(solution)/shard_map/ppermute | solution.py:81
  74.8 4.6 %collective-permute-start.9 = (bf16[64,256]{1,0:T(8,128)(2,1)S(1)}, bf16[64,256]{1,0:T(8,128)(2,1)S(1)}, u32[]{:S(2)}, u32[]{:S(2)}) collective-permute-start(bf16[64,256]{1,0:T(8,128)(2,1)S(1)} %collective-permute-done.7), channel_id=1, source_target_pairs={{0,32},{32,64},{64,96},{96,128},{128,160},{160,192},{192,224},{224... | collective-permute-start | bytes 98312 | tf_op jit(solution)/shard_map/ppermute | solution.py:76
  75.0 4.6 %collective-permute-start.10 = (bf16[64,256]{1,0:T(8,128)(2,1)S(1)}, bf16[64,256]{1,0:T(8,128)(2,1)S(1)}, u32[]{:S(2)}, u32[]{:S(2)}) collective-permute-start(bf16[64,256]{1,0:T(8,128)(2,1)S(1)} %collective-permute-done.8), channel_id=1, source_target_pairs={{0,480},{32,0},{64,32},{96,64},{128,96},{160,128},{192,160},{224,1... | collective-permute-start | bytes 98312 | tf_op jit(solution)/shard_map/ppermute | solution.py:81
  79.4 4.6 %collective-permute-start.11 = (bf16[64,256]{1,0:T(8,128)(2,1)S(1)}, bf16[64,256]{1,0:T(8,128)(2,1)S(1)}, u32[]{:S(2)}, u32[]{:S(2)}) collective-permute-start(bf16[64,256]{1,0:T(8,128)(2,1)S(1)} %collective-permute-done.9), channel_id=1, source_target_pairs={{0,32},{32,64},{64,96},{96,128},{128,160},{160,192},{192,224},{224... | collective-permute-start | bytes 98312 | tf_op jit(solution)/shard_map/ppermute | solution.py:76
  79.5 4.6 %collective-permute-start.12 = (bf16[64,256]{1,0:T(8,128)(2,1)S(1)}, bf16[64,256]{1,0:T(8,128)(2,1)S(1)}, u32[]{:S(2)}, u32[]{:S(2)}) collective-permute-start(bf16[64,256]{1,0:T(8,128)(2,1)S(1)} %collective-permute-done.10), channel_id=1, source_target_pairs={{0,480},{32,0},{64,32},{96,64},{128,96},{160,128},{192,160},{224,1... | collective-permute-start | bytes 98312 | tf_op jit(solution)/shard_map/ppermute | solution.py:81
  83.9 4.6 %collective-permute-start.13 = (bf16[64,256]{1,0:T(8,128)(2,1)S(1)}, bf16[64,256]{1,0:T(8,128)(2,1)S(1)}, u32[]{:S(2)}, u32[]{:S(2)}) collective-permute-start(bf16[64,256]{1,0:T(8,128)(2,1)S(1)} %collective-permute-done.11), channel_id=1, source_target_pairs={{0,32},{32,64},{64,96},{96,128},{128,160},{160,192},{192,224},{224... | collective-permute-start | bytes 98312 | tf_op jit(solution)/shard_map/ppermute | solution.py:76
  84.1 4.6 %collective-permute-start.14 = (bf16[64,256]{1,0:T(8,128)(2,1)S(1)}, bf16[64,256]{1,0:T(8,128)(2,1)S(1)}, u32[]{:S(2)}, u32[]{:S(2)}) collective-permute-start(bf16[64,256]{1,0:T(8,128)(2,1)S(1)} %collective-permute-done.12), channel_id=1, source_target_pairs={{0,480},{32,0},{64,32},{96,64},{128,96},{160,128},{192,160},{224,1... | collective-permute-start | bytes 98312 | tf_op jit(solution)/shard_map/ppermute | solution.py:81
  88.5 4.6 %collective-permute-start.15 = (bf16[64,256]{1,0:T(8,128)(2,1)S(1)}, bf16[64,256]{1,0:T(8,128)(2,1)S(1)}, u32[]{:S(2)}, u32[]{:S(2)}) collective-permute-start(bf16[64,256]{1,0:T(8,128)(2,1)S(1)} %collective-permute-done.13), channel_id=1, source_target_pairs={{0,32},{32,64},{64,96},{96,128},{128,160},{160,192},{192,224},{224... | collective-permute-start | bytes 98312 | tf_op jit(solution)/shard_map/ppermute | solution.py:76
  88.6 4.4 %copy-start.2 = (bf16[64,128]{1,0:T(8,128)(2,1)S(1)}, bf16[64,128]{1,0:T(8,128)(2,1)}, u32[]{:S(2)}) copy-start(bf16[64,128]{1,0:T(8,128)(2,1)} %param.6) | copy-start | bytes 49156
  124.7 12.5 %all-to-all-start.3 = ((bf16[32,2,256]{2,1,0:T(2,128)(2,1)}), bf16[32,2,256]{2,1,0:T(2,128)(2,1)S(1)}, u32[]{:S(2)}, u32[]{:S(2)}) async-start(bf16[32,2,256]{2,1,0:T(2,128)(2,1)} %broadcast_in_dim.23), calls=%async_computation.3 | async-start | bytes 65536 | tf_op jit(solution)/shard_map/all_to_all | solution.py:27
  128.5 43.8 %collective-permute-start.16 = (f32[64,128]{1,0:T(8,128)S(1)}, f32[64,128]{1,0:T(8,128)S(1)}, u32[]{:S(2)}, u32[]{:S(2)}) collective-permute-start(f32[64,128]{1,0:T(8,128)S(1)} %get-tuple-element.6), channel_id=1, source_target_pairs={{32,0},{64,32},{96,64},{128,96},{160,128},{192,160},{224,192},{256... | collective-permute-start | bytes 98312 | tf_op jit(solution)/shard_map/ppermute | solution.py:44
  137.2 5.2 %collective-permute-start.17 = (bf16[64,256]{1,0:T(8,128)(2,1)S(1)}, bf16[64,256]{1,0:T(8,128)(2,1)S(1)}, u32[]{:S(2)}, u32[]{:S(2)}) collective-permute-start(bf16[64,256]{1,0:T(8,128)(2,1)S(1)} %reshape.27), channel_id=1, source_target_pairs={{0,32},{32,64},{64,96},{96,128},{128,160},{160,192},{192,224},{224... | collective-permute-start | bytes 98312 | tf_op jit(solution)/shard_map/ppermute | solution.py:76
  141.3 3.3 %collective-permute-start.18 = (bf16[64,256]{1,0:T(8,128)(2,1)S(1)}, bf16[64,256]{1,0:T(8,128)(2,1)S(1)}, u32[]{:S(2)}, u32[]{:S(2)}) collective-permute-start(bf16[64,256]{1,0:T(8,128)(2,1)S(1)} %reshape.27), channel_id=1, source_target_pairs={{0,480},{32,0},{64,32},{96,64},{128,96},{160,128},{192,160},{224,1... | collective-permute-start | bytes 98312 | tf_op jit(solution)/shard_map/ppermute | solution.py:81
  142.4 3.3 %collective-permute-start.19 = (bf16[64,256]{1,0:T(8,128)(2,1)S(1)}, bf16[64,256]{1,0:T(8,128)(2,1)S(1)}, u32[]{:S(2)}, u32[]{:S(2)}) collective-permute-start(bf16[64,256]{1,0:T(8,128)(2,1)S(1)} %collective-permute-done.17), channel_id=1, source_target_pairs={{0,32},{32,64},{64,96},{96,128},{128,160},{160,192},{192,224},{224... | collective-permute-start | bytes 98312 | tf_op jit(solution)/shard_map/ppermute | solution.py:76
  144.7 3.6 %collective-permute-start.20 = (bf16[64,256]{1,0:T(8,128)(2,1)S(1)}, bf16[64,256]{1,0:T(8,128)(2,1)S(1)}, u32[]{:S(2)}, u32[]{:S(2)}) collective-permute-start(bf16[64,256]{1,0:T(8,128)(2,1)S(1)} %collective-permute-done.18), channel_id=1, source_target_pairs={{0,480},{32,0},{64,32},{96,64},{128,96},{160,128},{192,160},{224,1... | collective-permute-start | bytes 98312 | tf_op jit(solution)/shard_map/ppermute | solution.py:81
  145.7 3.8 %collective-permute-start.21 = (bf16[64,256]{1,0:T(8,128)(2,1)S(1)}, bf16[64,256]{1,0:T(8,128)(2,1)S(1)}, u32[]{:S(2)}, u32[]{:S(2)}) collective-permute-start(bf16[64,256]{1,0:T(8,128)(2,1)S(1)} %collective-permute-done.19), channel_id=1, source_target_pairs={{0,32},{32,64},{64,96},{96,128},{128,160},{160,192},{192,224},{224... | collective-permute-start | bytes 98312 | tf_op jit(solution)/shard_map/ppermute | solution.py:76
  148.3 3.3 %collective-permute-start.22 = (bf16[64,256]{1,0:T(8,128)(2,1)S(1)}, bf16[64,256]{1,0:T(8,128)(2,1)S(1)}, u32[]{:S(2)}, u32[]{:S(2)}) collective-permute-start(bf16[64,256]{1,0:T(8,128)(2,1)S(1)} %collective-permute-done.20), channel_id=1, source_target_pairs={{0,480},{32,0},{64,32},{96,64},{128,96},{160,128},{192,160},{224,1... | collective-permute-start | bytes 98312 | tf_op jit(solution)/shard_map/ppermute | solution.py:81
  149.5 4.6 %collective-permute-start.23 = (bf16[64,256]{1,0:T(8,128)(2,1)S(1)}, bf16[64,256]{1,0:T(8,128)(2,1)S(1)}, u32[]{:S(2)}, u32[]{:S(2)}) collective-permute-start(bf16[64,256]{1,0:T(8,128)(2,1)S(1)} %collective-permute-done.21), channel_id=1, source_target_pairs={{0,32},{32,64},{64,96},{96,128},{128,160},{160,192},{192,224},{224... | collective-permute-start | bytes 98312 | tf_op jit(solution)/shard_map/ppermute | solution.py:76
  151.7 3.3 %collective-permute-start.24 = (bf16[64,256]{1,0:T(8,128)(2,1)S(1)}, bf16[64,256]{1,0:T(8,128)(2,1)S(1)}, u32[]{:S(2)}, u32[]{:S(2)}) collective-permute-start(bf16[64,256]{1,0:T(8,128)(2,1)S(1)} %collective-permute-done.22), channel_id=1, source_target_pairs={{0,480},{32,0},{64,32},{96,64},{128,96},{160,128},{192,160},{224,1... | collective-permute-start | bytes 98312 | tf_op jit(solution)/shard_map/ppermute | solution.py:81
  154.1 4.6 %collective-permute-start.25 = (bf16[64,256]{1,0:T(8,128)(2,1)S(1)}, bf16[64,256]{1,0:T(8,128)(2,1)S(1)}, u32[]{:S(2)}, u32[]{:S(2)}) collective-permute-start(bf16[64,256]{1,0:T(8,128)(2,1)S(1)} %collective-permute-done.23), channel_id=1, source_target_pairs={{0,32},{32,64},{64,96},{96,128},{128,160},{160,192},{192,224},{224... | collective-permute-start | bytes 98312 | tf_op jit(solution)/shard_map/ppermute | solution.py:76
  155.0 3.8 %collective-permute-start.26 = (bf16[64,256]{1,0:T(8,128)(2,1)S(1)}, bf16[64,256]{1,0:T(8,128)(2,1)S(1)}, u32[]{:S(2)}, u32[]{:S(2)}) collective-permute-start(bf16[64,256]{1,0:T(8,128)(2,1)S(1)} %collective-permute-done.24), channel_id=1, source_target_pairs={{0,480},{32,0},{64,32},{96,64},{128,96},{160,128},{192,160},{224,1... | collective-permute-start | bytes 98312 | tf_op jit(solution)/shard_map/ppermute | solution.py:81
  158.7 4.6 %collective-permute-start.27 = (bf16[64,256]{1,0:T(8,128)(2,1)S(1)}, bf16[64,256]{1,0:T(8,128)(2,1)S(1)}, u32[]{:S(2)}, u32[]{:S(2)}) collective-permute-start(bf16[64,256]{1,0:T(8,128)(2,1)S(1)} %collective-permute-done.25), channel_id=1, source_target_pairs={{0,32},{32,64},{64,96},{96,128},{128,160},{160,192},{192,224},{224... | collective-permute-start | bytes 98312 | tf_op jit(solution)/shard_map/ppermute | solution.py:76
  158.8 4.6 %collective-permute-start.28 = (bf16[64,256]{1,0:T(8,128)(2,1)S(1)}, bf16[64,256]{1,0:T(8,128)(2,1)S(1)}, u32[]{:S(2)}, u32[]{:S(2)}) collective-permute-start(bf16[64,256]{1,0:T(8,128)(2,1)S(1)} %collective-permute-done.26), channel_id=1, source_target_pairs={{0,480},{32,0},{64,32},{96,64},{128,96},{160,128},{192,160},{224,1... | collective-permute-start | bytes 98312 | tf_op jit(solution)/shard_map/ppermute | solution.py:81
  163.2 4.6 %collective-permute-start.29 = (bf16[64,256]{1,0:T(8,128)(2,1)S(1)}, bf16[64,256]{1,0:T(8,128)(2,1)S(1)}, u32[]{:S(2)}, u32[]{:S(2)}) collective-permute-start(bf16[64,256]{1,0:T(8,128)(2,1)S(1)} %collective-permute-done.27), channel_id=1, source_target_pairs={{0,32},{32,64},{64,96},{96,128},{128,160},{160,192},{192,224},{224... | collective-permute-start | bytes 98312 | tf_op jit(solution)/shard_map/ppermute | solution.py:76
  163.4 4.6 %collective-permute-start.30 = (bf16[64,256]{1,0:T(8,128)(2,1)S(1)}, bf16[64,256]{1,0:T(8,128)(2,1)S(1)}, u32[]{:S(2)}, u32[]{:S(2)}) collective-permute-start(bf16[64,256]{1,0:T(8,128)(2,1)S(1)} %collective-permute-done.28), channel_id=1, source_target_pairs={{0,480},{32,0},{64,32},{96,64},{128,96},{160,128},{192,160},{224,1... | collective-permute-start | bytes 98312 | tf_op jit(solution)/shard_map/ppermute | solution.py:81
  167.8 4.6 %collective-permute-start.31 = (bf16[64,256]{1,0:T(8,128)(2,1)S(1)}, bf16[64,256]{1,0:T(8,128)(2,1)S(1)}, u32[]{:S(2)}, u32[]{:S(2)}) collective-permute-start(bf16[64,256]{1,0:T(8,128)(2,1)S(1)} %collective-permute-done.29), channel_id=1, source_target_pairs={{0,32},{32,64},{64,96},{96,128},{128,160},{160,192},{192,224},{224... | collective-permute-start | bytes 98312 | tf_op jit(solution)/shard_map/ppermute | solution.py:76
  203.9 12.5 %all-to-all-start.5 = ((bf16[32,2,256]{2,1,0:T(2,128)(2,1)}), bf16[32,2,256]{2,1,0:T(2,128)(2,1)S(1)}, u32[]{:S(2)}, u32[]{:S(2)}) async-start(bf16[32,2,256]{2,1,0:T(2,128)(2,1)} %broadcast_in_dim.24), calls=%async_computation.5 | async-start | bytes 65536 | tf_op jit(solution)/shard_map/all_to_all | solution.py:27
  207.9 43.7 %collective-permute-start.32 = (f32[64,128]{1,0:T(8,128)S(1)}, f32[64,128]{1,0:T(8,128)S(1)}, u32[]{:S(2)}, u32[]{:S(2)}) collective-permute-start(f32[64,128]{1,0:T(8,128)S(1)} %get-tuple-element.8), channel_id=1, source_target_pairs={{32,0},{64,32},{96,64},{128,96},{160,128},{192,160},{224,192},{256... | collective-permute-start | bytes 98312 | tf_op jit(solution)/shard_map/ppermute | solution.py:44
  216.5 5.2 %collective-permute-start.33 = (bf16[64,256]{1,0:T(8,128)(2,1)S(1)}, bf16[64,256]{1,0:T(8,128)(2,1)S(1)}, u32[]{:S(2)}, u32[]{:S(2)}) collective-permute-start(bf16[64,256]{1,0:T(8,128)(2,1)S(1)} %reshape.28), channel_id=1, source_target_pairs={{0,32},{32,64},{64,96},{96,128},{128,160},{160,192},{192,224},{224... | collective-permute-start | bytes 98312 | tf_op jit(solution)/shard_map/ppermute | solution.py:76
  220.6 3.3 %collective-permute-start.34 = (bf16[64,256]{1,0:T(8,128)(2,1)S(1)}, bf16[64,256]{1,0:T(8,128)(2,1)S(1)}, u32[]{:S(2)}, u32[]{:S(2)}) collective-permute-start(bf16[64,256]{1,0:T(8,128)(2,1)S(1)} %reshape.28), channel_id=1, source_target_pairs={{0,480},{32,0},{64,32},{96,64},{128,96},{160,128},{192,160},{224,1... | collective-permute-start | bytes 98312 | tf_op jit(solution)/shard_map/ppermute | solution.py:81
  221.6 3.3 %collective-permute-start.35 = (bf16[64,256]{1,0:T(8,128)(2,1)S(1)}, bf16[64,256]{1,0:T(8,128)(2,1)S(1)}, u32[]{:S(2)}, u32[]{:S(2)}) collective-permute-start(bf16[64,256]{1,0:T(8,128)(2,1)S(1)} %collective-permute-done.33), channel_id=1, source_target_pairs={{0,32},{32,64},{64,96},{96,128},{128,160},{160,192},{192,224},{224... | collective-permute-start | bytes 98312 | tf_op jit(solution)/shard_map/ppermute | solution.py:76
  223.9 3.6 %collective-permute-start.36 = (bf16[64,256]{1,0:T(8,128)(2,1)S(1)}, bf16[64,256]{1,0:T(8,128)(2,1)S(1)}, u32[]{:S(2)}, u32[]{:S(2)}) collective-permute-start(bf16[64,256]{1,0:T(8,128)(2,1)S(1)} %collective-permute-done.34), channel_id=1, source_target_pairs={{0,480},{32,0},{64,32},{96,64},{128,96},{160,128},{192,160},{224,1... | collective-permute-start | bytes 98312 | tf_op jit(solution)/shard_map/ppermute | solution.py:81
  225.0 3.8 %collective-permute-start.37 = (bf16[64,256]{1,0:T(8,128)(2,1)S(1)}, bf16[64,256]{1,0:T(8,128)(2,1)S(1)}, u32[]{:S(2)}, u32[]{:S(2)}) collective-permute-start(bf16[64,256]{1,0:T(8,128)(2,1)S(1)} %collective-permute-done.35), channel_id=1, source_target_pairs={{0,32},{32,64},{64,96},{96,128},{128,160},{160,192},{192,224},{224... | collective-permute-start | bytes 98312 | tf_op jit(solution)/shard_map/ppermute | solution.py:76
  227.6 3.3 %collective-permute-start.38 = (bf16[64,256]{1,0:T(8,128)(2,1)S(1)}, bf16[64,256]{1,0:T(8,128)(2,1)S(1)}, u32[]{:S(2)}, u32[]{:S(2)}) collective-permute-start(bf16[64,256]{1,0:T(8,128)(2,1)S(1)} %collective-permute-done.36), channel_id=1, source_target_pairs={{0,480},{32,0},{64,32},{96,64},{128,96},{160,128},{192,160},{224,1... | collective-permute-start | bytes 98312 | tf_op jit(solution)/shard_map/ppermute | solution.py:81
  228.8 4.6 %collective-permute-start.39 = (bf16[64,256]{1,0:T(8,128)(2,1)S(1)}, bf16[64,256]{1,0:T(8,128)(2,1)S(1)}, u32[]{:S(2)}, u32[]{:S(2)}) collective-permute-start(bf16[64,256]{1,0:T(8,128)(2,1)S(1)} %collective-permute-done.37), channel_id=1, source_target_pairs={{0,32},{32,64},{64,96},{96,128},{128,160},{160,192},{192,224},{224... | collective-permute-start | bytes 98312 | tf_op jit(solution)/shard_map/ppermute | solution.py:76
  230.9 3.3 %collective-permute-start.40 = (bf16[64,256]{1,0:T(8,128)(2,1)S(1)}, bf16[64,256]{1,0:T(8,128)(2,1)S(1)}, u32[]{:S(2)}, u32[]{:S(2)}) collective-permute-start(bf16[64,256]{1,0:T(8,128)(2,1)S(1)} %collective-permute-done.38), channel_id=1, source_target_pairs={{0,480},{32,0},{64,32},{96,64},{128,96},{160,128},{192,160},{224,1... | collective-permute-start | bytes 98312 | tf_op jit(solution)/shard_map/ppermute | solution.py:81
  233.4 4.6 %collective-permute-start.41 = (bf16[64,256]{1,0:T(8,128)(2,1)S(1)}, bf16[64,256]{1,0:T(8,128)(2,1)S(1)}, u32[]{:S(2)}, u32[]{:S(2)}) collective-permute-start(bf16[64,256]{1,0:T(8,128)(2,1)S(1)} %collective-permute-done.39), channel_id=1, source_target_pairs={{0,32},{32,64},{64,96},{96,128},{128,160},{160,192},{192,224},{224... | collective-permute-start | bytes 98312 | tf_op jit(solution)/shard_map/ppermute | solution.py:76
  234.3 3.8 %collective-permute-start.42 = (bf16[64,256]{1,0:T(8,128)(2,1)S(1)}, bf16[64,256]{1,0:T(8,128)(2,1)S(1)}, u32[]{:S(2)}, u32[]{:S(2)}) collective-permute-start(bf16[64,256]{1,0:T(8,128)(2,1)S(1)} %collective-permute-done.40), channel_id=1, source_target_pairs={{0,480},{32,0},{64,32},{96,64},{128,96},{160,128},{192,160},{224,1... | collective-permute-start | bytes 98312 | tf_op jit(solution)/shard_map/ppermute | solution.py:81
  237.9 4.6 %collective-permute-start.43 = (bf16[64,256]{1,0:T(8,128)(2,1)S(1)}, bf16[64,256]{1,0:T(8,128)(2,1)S(1)}, u32[]{:S(2)}, u32[]{:S(2)}) collective-permute-start(bf16[64,256]{1,0:T(8,128)(2,1)S(1)} %collective-permute-done.41), channel_id=1, source_target_pairs={{0,32},{32,64},{64,96},{96,128},{128,160},{160,192},{192,224},{224... | collective-permute-start | bytes 98312 | tf_op jit(solution)/shard_map/ppermute | solution.py:76
  238.1 4.6 %collective-permute-start.44 = (bf16[64,256]{1,0:T(8,128)(2,1)S(1)}, bf16[64,256]{1,0:T(8,128)(2,1)S(1)}, u32[]{:S(2)}, u32[]{:S(2)}) collective-permute-start(bf16[64,256]{1,0:T(8,128)(2,1)S(1)} %collective-permute-done.42), channel_id=1, source_target_pairs={{0,480},{32,0},{64,32},{96,64},{128,96},{160,128},{192,160},{224,1... | collective-permute-start | bytes 98312 | tf_op jit(solution)/shard_map/ppermute | solution.py:81
  242.5 4.6 %collective-permute-start.45 = (bf16[64,256]{1,0:T(8,128)(2,1)S(1)}, bf16[64,256]{1,0:T(8,128)(2,1)S(1)}, u32[]{:S(2)}, u32[]{:S(2)}) collective-permute-start(bf16[64,256]{1,0:T(8,128)(2,1)S(1)} %collective-permute-done.43), channel_id=1, source_target_pairs={{0,32},{32,64},{64,96},{96,128},{128,160},{160,192},{192,224},{224... | collective-permute-start | bytes 98312 | tf_op jit(solution)/shard_map/ppermute | solution.py:76
  242.7 4.6 %collective-permute-start.46 = (bf16[64,256]{1,0:T(8,128)(2,1)S(1)}, bf16[64,256]{1,0:T(8,128)(2,1)S(1)}, u32[]{:S(2)}, u32[]{:S(2)}) collective-permute-start(bf16[64,256]{1,0:T(8,128)(2,1)S(1)} %collective-permute-done.44), channel_id=1, source_target_pairs={{0,480},{32,0},{64,32},{96,64},{128,96},{160,128},{192,160},{224,1... | collective-permute-start | bytes 98312 | tf_op jit(solution)/shard_map/ppermute | solution.py:81
  247.0 4.6 %collective-permute-start.47 = (bf16[64,256]{1,0:T(8,128)(2,1)S(1)}, bf16[64,256]{1,0:T(8,128)(2,1)S(1)}, u32[]{:S(2)}, u32[]{:S(2)}) collective-permute-start(bf16[64,256]{1,0:T(8,128)(2,1)S(1)} %collective-permute-done.45), channel_id=1, source_target_pairs={{0,32},{32,64},{64,96},{96,128},{128,160},{160,192},{192,224},{224... | collective-permute-start | bytes 98312 | tf_op jit(solution)/shard_map/ppermute | solution.py:76
